TPU v7x, 32 devices: a whole 2x2x4 slice. The times are simulated.
32 devices in a mesh: wide: 32 (over z, y, x, core), tensor: 1.
Axes of the slice: x: 2, y: 2, z: 4, core: 2. Of those that a mesh axis runs over, the one named last changes fastest.
Arguments:
- hidden: bfloat16 [49152, 3072], P('wide', 'tensor'), may hold values from -6 to 6
- modulation: float32 [2, 3072], P(None, 'tensor'), may hold values from -3 to 3
- final_weight: bfloat16 [3072, 64], P('tensor'), may hold values from -0.109375 to 0.109375
- noisy: float32 [49152, 64], P('wide'), may hold values from -6 to 6
- step_index: int32 [1], replicated, may hold values from 1 to 28
- slab_table: int32 [768], P('wide'), may hold values from 0 to 31, as said below
- conv_in_weight: bfloat16 [144, 512], P(None, 'tensor'), may hold values from -0.5 to 0.5
- conv_in_bias: float32 [512], P('tensor'), may hold values from -3 to 3
- conv1_weight: bfloat16 [9, 512, 512], replicated, may hold values from -0.09375 to 0.09375
- conv1_bias: float32 [512], replicated, may hold values from -3 to 3
Outputs:
- decoder_features: bfloat16 [1536, 512, 128], P('wide', 'tensor')
- residual_branch: bfloat16 [1536, 512, 128], P('wide', 'tensor')
Inputs may be any that keep to these rules, and one draw needn't show every extreme that they name: There are 24 distinct offsets o_j, one per local row j, with slab_table[w * 24 + j] = (w - o_j) modulo the number of wide devices: each slab receives each local row index from exactly one wide device, and the rows of one device go to distinct slabs. One of the offsets is half the number of wide devices (rounded down).
All inputs are finite; a program needn't handle non-finite values.
Results may differ from a plain program's by a relative error of at most 0.012.
Values may be sent and summed in bfloat16 or wider, within the bound.
A program may use at most 192 MiB of HBM per device.

v0:
```python
import jax
import jax.numpy as jnp
from jax import lax
from jax.sharding import PartitionSpec as P

D = 3072
LC = 16
GRID = 64
STEPS = 28


shift_value = 3.0
norm_eps = 1e-06


def padded_2(value, sides, width):
    for axis, dim in sides:
        count, length = (lax.axis_size(axis), value.shape[dim])
        up = [(i, (i + 1) % count) for i in range(count - 1)]
        down = [(j, i) for i, j in up]
        last = lax.slice_in_dim(value, length - width, length, axis=dim)
        first = lax.slice_in_dim(value, 0, width, axis=dim)
        before = lax.ppermute(last, axis, up)
        after = lax.ppermute(first, axis, down)
        value = jnp.concatenate([before, value, after], axis=dim)
    return value


def edge_masks(first_row, count, height):
    global_rows = first_row + jnp.arange(count, dtype=jnp.int32)
    upper = (global_rows % height != 0).astype(jnp.float32)
    lower = (global_rows % height != height - 1).astype(jnp.float32)
    return (upper, jnp.ones_like(upper), lower)


def conv_input_rows(latent, weight, bias, first_row, count, channels):
    width = latent.shape[1] // channels
    planes = latent.reshape(latent.shape[0], width, channels)
    padded = jnp.pad(planes, ((0, 0), (1, 1), (0, 0)))
    masks = edge_masks(first_row, count, width)
    pieces = []
    for row_off in range(3):
        keep = masks[row_off].astype(jnp.bfloat16)[:, None, None]
        for col_off in range(3):
            pieces.append(padded[row_off : row_off + count, col_off : col_off + width, :] * keep)
    patches = jnp.concatenate(pieces, axis=-1)
    return jnp.einsum("rwk,ko->rwo", patches, weight, preferred_element_type=jnp.float32) + bias


def conv_three(total, inputs, weights, first_row, count):
    width = inputs.shape[2]
    padded = jnp.pad(inputs, ((0, 0), (0, 0), (1, 1)))
    masks = edge_masks(first_row, count, width)
    for row_off in range(3):
        keep = masks[row_off][:, None, None]
        for col_off in range(3):
            window = padded[row_off : row_off + count, :, col_off : col_off + width]
            term = jnp.einsum(
                "rkw,ko->row",
                window,
                weights[3 * row_off + col_off],
                preferred_element_type=jnp.float32,
            )
            total = total + keep * term
    return total


def shards(
    hidden,
    modulation,
    final_weight,
    noisy,
    step_index,
    slab_table,
    conv_in_weight,
    conv_in_bias,
    conv1_weight,
    conv1_bias,
):
    feats = hidden.astype(jnp.float32)
    weight_f = final_weight.astype(jnp.float32)
    width_all = D
    first_sum, square_sum = lax.psum(
        (jnp.sum(feats, axis=-1), jnp.sum(feats * feats, axis=-1)), "tensor"
    )
    mean = first_sum / width_all
    rstd = 1.0 / jnp.sqrt(square_sum / width_all - mean * mean + norm_eps)
    normed = (feats - mean[:, None]) * rstd[:, None] * (1.0 + modulation[1]) + modulation[0]
    partial_proj = jnp.dot(normed, weight_f, precision=lax.Precision.HIGHEST)
    velocity = lax.psum(partial_proj, "tensor")
    frac = step_index[0].astype(jnp.float32) / STEPS
    sigma = shift_value * frac / (1.0 + (shift_value - 1.0) * frac)
    clean = (noisy - sigma * velocity).astype(jnp.bfloat16)
    rows_here = slab_table.shape[0]
    token_rows = clean.reshape(rows_here, -1)
    slabs = lax.axis_size("wide")
    slab_here = lax.axis_index("wide")
    slab_ids = jnp.arange(slabs, dtype=jnp.int32)
    outgoing = (slab_ids[:, None] == slab_table[None, :]).astype(jnp.bfloat16)
    sendbuf = jnp.dot(outgoing, token_rows, preferred_element_type=jnp.float32).astype(jnp.bfloat16)
    received = lax.all_to_all(sendbuf, "wide", split_axis=0, concat_axis=0, tiled=True)
    source = (2 * slab_here - slab_table) % slabs
    incoming = (source[:, None] == slab_ids[None, :]).astype(jnp.bfloat16)
    slab_rows = jnp.dot(incoming, received, preferred_element_type=jnp.float32).astype(jnp.bfloat16)
    grid_side = GRID
    channels = LC
    pixel_rows = (
        slab_rows.reshape(rows_here, grid_side, 2, 2, channels)
        .transpose(0, 2, 1, 3, 4)
        .reshape(2 * rows_here, 4 * grid_side * channels // 2)
    )
    depth = 2
    latent = padded_2(pixel_rows, (("wide", 0),), depth)
    slab_height = 2 * rows_here
    conv_rows = slab_height + 2 * (depth - 1)
    first_conv = slab_here * slab_height - (depth - 1)
    first = conv_input_rows(latent, conv_in_weight, conv_in_bias, first_conv, conv_rows, channels)
    features = first.astype(jnp.bfloat16).transpose(0, 2, 1)
    activated = jax.nn.silu(features.astype(jnp.float32)).astype(jnp.bfloat16)
    decoder_features = features[depth - 1 : depth - 1 + slab_height]
    local_out = conv_in_weight.shape[1]
    tensor_here = lax.axis_index("tensor")
    pixel_width = activated.shape[2]
    columns = lax.dynamic_slice_in_dim(conv1_weight, tensor_here * local_out, local_out, 2)
    bias_part = lax.dynamic_slice_in_dim(conv1_bias, tensor_here * local_out, local_out, 0)
    first_out = slab_here * slab_height
    gathered = lax.all_gather(activated, "tensor", axis=1, tiled=True)
    start_total = jnp.zeros((slab_height, local_out, pixel_width), jnp.float32)
    summed = conv_three(start_total, gathered, columns, first_out, slab_height)
    residual_branch = (summed + bias_part[None, :, None]).astype(jnp.bfloat16)
    return (decoder_features, residual_branch)


def solution(mesh):
    return jax.shard_map(
        shards,
        mesh=mesh,
        in_specs=(
            P("wide", "tensor"),
            P(None, "tensor"),
            P("tensor", None),
            P("wide", None),
            P(),
            P("wide"),
            P(None, "tensor"),
            P("tensor"),
            P(),
            P(),
        ),
        out_specs=(P("wide", "tensor", None), P("wide", "tensor", None)),
        check_vma=False,
    )
```

profile of v0, /device:TPU:0, one launch (start us, length us, event | category | flops | bytes accessed | tf_op | source)
XLA Modules:
  0.0 168.3 jit_solution(17253016311994126917)
XLA Ops:
  0.6 0.0 copy-start
  1.5 6.7 %convert_reduce_fusion = (f32[1536]{0:T(1024)S(1)}, f32[1536]{0:T(1024)S(1)}) fusion(bf16[1536,3072]{1,0:T(8,128)(2,1)} %param.10), kind=kLoop, calls=%fused_computation.2 | loop fusion | flops 18871296 | bytes 9449472 | tf_op jit(solution)/shard_map/reduce_sum | solution.py:84
  8.2 0.8 slice_add_fusion
  9.1 14.3 %fusion.41 = bf16[1536,64]{0,1:T(8,128)(2,1)S(1)} fusion(f32[1536,64]{0,1:T(8,128)} %param.13, bf16[3072,64]{0,1:T(8,128)(2,1)S(1)} %copy-done, bf16[1536,3072]{1,0:T(8,128)(2,1)S(1)} %copy-done.3, f32[3072]{0:T(1024)S(1)} %bitcast.67, f32[3072]{0:T(1024)S(1)} %bitcast.66, f32[1536]{0:T(1024)S(1)} %get-tuple-element.17, f32[1536]{0:T(1024)S(1)} %get-tuple-element.16, ...), kind=kOutput, calls=%fused_computation.46 | convolution fusion | flops 3647766528 | bytes 10457092 | tf_op jit(solution)/shard_map/dot_general | solution.py:89
  23.4 0.2 copy.42
  23.6 0.4 reshape.88
  24.0 0.2 fusion.28
  24.2 0.5 broadcast.181
  24.7 0.8 reduce
  25.5 0.9 reshape.100
  26.4 7.3 %all-to-all-start = ((bf16[32,2,2048]{2,1,0:T(2,128)(2,1)}), bf16[32,2,2048]{2,1,0:T(2,128)(2,1)S(1)}, u32[]{:S(2)}, u32[]{:S(2)}) async-start(bf16[32,2,2048]{2,1,0:T(2,128)(2,1)} %reshape.100), calls=%async_computation | async-start | bytes 524288 | tf_op jit(solution)/shard_map/all_to_all | solution.py:101
  33.8 10.5 %all-to-all-done = bf16[32,2,2048]{2,1,0:T(2,128)(2,1)S(1)} async-done(((bf16[32,2,2048]{2,1,0:T(2,128)(2,1)}), bf16[32,2,2048]{2,1,0:T(2,128)(2,1)S(1)}, u32[]{:S(2)}, u32[]{:S(2)}) %all-to-all-start) | async-done | bytes 262176 | tf_op jit(solution)/shard_map/all_to_all | solution.py:101
  44.3 0.3 reshape.101
  44.6 0.4 convolution_convert_fusion.1
  45.0 1.3 reshape.89
  46.3 0.1 fusion.92
  46.5 0.1 slice.109
  46.6 1.8 %collective-permute-start = (bf16[2,2048]{1,0:T(2,128)(2,1)S(1)}, bf16[2,2048]{1,0:T(2,128)(2,1)S(1)}, u32[]{:S(2)}, u32[]{:S(2)}) collective-permute-start(bf16[2,2048]{1,0:T(2,128)(2,1)S(1)} %slice.109), channel_id=1, source_target_pairs={{0,1},{1,2},{2,3},{3,4},{4,5},{5,6},{6,7},{7,8},{8,9},{9,10},{10,1... | collective-permute-start | bytes 24584 | tf_op jit(solution)/shard_map/ppermute | solution.py:23
  48.5 0.1 slice.111
  48.6 1.5 collective-permute-start.1
  50.1 1.7 copy.45
  51.7 0.6 copy.48
  52.4 0.1 concatenate.19
  52.5 0.1 copy.47
  52.6 0.1 concatenate.21
  52.7 0.1 copy.49
  52.8 0.1 pad_maximum_fusion
  52.8 0.2 fusion.67
  53.0 0.1 fusion.76
  53.2 0.2 fusion.69
  53.4 0.2 fusion.70
  53.6 0.1 fusion.71
  53.7 0.2 fusion.73
  54.0 0.1 fusion.77
  54.1 0.2 fusion.75
  54.4 5.3 %fusion.9 = (bf16[50,512,128]{1,2,0:T(8,128)(2,1)S(1)}, bf16[50,512,128]{1,2,0:T(8,128)(2,1)S(1)}) fusion(f32[512]{0:T(512)S(1)} %copy-done.6, bf16[50,128,144]{1,2,0:T(8,128)(2,1)S(1)} %fusion.75, bf16[144,512]{1,0:T(8,128)(2,1)} %param.16), kind=kOutput, calls=%fused_computation.13 | convolution fusion | flops 969932800 | bytes 15099904 | tf_op jit(solution)/shard_map/rwk,ko->rwo/dot_general | solution.py:47
  59.7 6.4 %fusion.22 = f32[48,128,512]{2,1,0:T(8,128)} fusion(bf16[50,512,128]{1,2,0:T(8,128)(2,1)S(1)} %get-tuple-element.18, bf16[9,512,512]{2,1,0:T(8,128)(2,1)S(1)} %bitcast.65), kind=kOutput, calls=%fused_computation.29 | convolution fusion | flops 3221225472 | bytes 19660800 | tf_op jit(solution)/shard_map/rkw,ko->row/dot_general | solution.py:58
  66.1 6.4 %fusion.20 = f32[48,128,512]{2,1,0:T(8,128)} fusion(bf16[50,512,128]{1,2,0:T(8,128)(2,1)S(1)} %get-tuple-element.18, bf16[9,512,512]{2,1,0:T(8,128)(2,1)S(1)} %bitcast.65), kind=kOutput, calls=%fused_computation.27 | convolution fusion | flops 3221225472 | bytes 19660800 | tf_op jit(solution)/shard_map/rkw,ko->row/dot_general | solution.py:58
  72.5 6.6 %fusion.18 = f32[48,128,512]{2,1,0:T(8,128)} fusion(bf16[50,512,128]{1,2,0:T(8,128)(2,1)S(1)} %get-tuple-element.18, bf16[9,512,512]{2,1,0:T(8,128)(2,1)S(1)} %bitcast.65), kind=kOutput, calls=%fused_computation.25 | convolution fusion | flops 3221225472 | bytes 19660800 | tf_op jit(solution)/shard_map/rkw,ko->row/dot_general | solution.py:58
  79.0 6.3 %fusion.16 = f32[48,128,512]{2,1,0:T(8,128)} fusion(bf16[50,512,128]{1,2,0:T(8,128)(2,1)S(1)} %get-tuple-element.18, bf16[9,512,512]{2,1,0:T(8,128)(2,1)S(1)} %bitcast.65), kind=kOutput, calls=%fused_computation.23 | convolution fusion | flops 3221225472 | bytes 19660800 | tf_op jit(solution)/shard_map/rkw,ko->row/dot_general | solution.py:58
  85.4 6.4 %fusion.14 = f32[48,128,512]{2,1,0:T(8,128)} fusion(bf16[50,512,128]{1,2,0:T(8,128)(2,1)S(1)} %get-tuple-element.18, bf16[9,512,512]{2,1,0:T(8,128)(2,1)S(1)} %bitcast.65), kind=kOutput, calls=%fused_computation.21 | convolution fusion | flops 3221225472 | bytes 19660800 | tf_op jit(solution)/shard_map/rkw,ko->row/dot_general | solution.py:58
  91.7 6.4 %fusion.48 = f32[48,128,512]{2,1,0:T(8,128)} fusion(bf16[50,512,128]{1,2,0:T(8,128)(2,1)S(1)} %get-tuple-element.18, bf16[9,512,512]{2,1,0:T(8,128)(2,1)S(1)} %bitcast.65), kind=kOutput, calls=%fused_computation.57 | convolution fusion | flops 3221225472 | bytes 19660800 | tf_op jit(solution)/shard_map/rkw,ko->row/dot_general | solution.py:58
  98.1 6.4 %fusion.52 = f32[48,128,512]{2,1,0:T(8,128)} fusion(bf16[50,512,128]{1,2,0:T(8,128)(2,1)S(1)} %get-tuple-element.18, bf16[9,512,512]{2,1,0:T(8,128)(2,1)S(1)} %bitcast.65), kind=kOutput, calls=%fused_computation.61 | convolution fusion | flops 3221225472 | bytes 19660800 | tf_op jit(solution)/shard_map/rkw,ko->row/dot_general | solution.py:58
  104.5 6.4 %fusion.24 = f32[48,128,512]{2,1,0:T(8,128)} fusion(bf16[50,512,128]{1,2,0:T(8,128)(2,1)S(1)} %get-tuple-element.18, bf16[9,512,512]{2,1,0:T(8,128)(2,1)S(1)} %bitcast.65), kind=kOutput, calls=%fused_computation.31 | convolution fusion | flops 3221225472 | bytes 19660800 | tf_op jit(solution)/shard_map/rkw,ko->row/dot_general | solution.py:58
  110.9 3.4 %slice.141 = bf16[48,512,128]{1,2,0:T(8,128)(2,1)} slice(bf16[50,512,128]{1,2,0:T(8,128)(2,1)S(1)} %get-tuple-element.19), slice={[1:49], [0:512], [0:128]} | slice | bytes 12582912 | tf_op jit(solution)/shard_map/slice | solution.py:120
  114.4 8.6 %copy.54 = bf16[48,512,128]{2,1,0:T(8,128)(2,1)} copy(bf16[48,512,128]{1,2,0:T(8,128)(2,1)} %slice.141) | data formatting | bytes 12582912
  123.0 36.7 %fusion.26 = bf16[48,512,128]{1,2,0:T(8,128)(2,1)} fusion(f32[512]{0:T(512)S(1)} %copy-done.4, f32[48,128,512]{2,1,0:T(8,128)} %fusion.14, f32[48,128,512]{2,1,0:T(8,128)} %fusion.16, f32[48]{0:T(128)S(1)} %get-tuple-element.20, f32[48,128,512]{2,1,0:T(8,128)} %fusion.18, f32[48,128,512]{2,1,0:T(8,128)} %fusion.48, f32[48,128,512]{2,1,0:T(8,128)} %fusion.20, ...), kind=kOutput, calls=%fused_computation.33 | convolution fusion | flops 3265265664 | bytes 114035072 | tf_op jit(solution)/shard_map/rkw,ko->row/dot_general | solution.py:58
  159.7 8.6 %copy.55 = bf16[48,512,128]{2,1,0:T(8,128)(2,1)} copy(bf16[48,512,128]{1,2,0:T(8,128)(2,1)} %fusion.26) | data formatting | bytes 12582912
  (28 shorter events, 0.2 us)
Async XLA Ops:
  0.6 8.5 %copy-start = (bf16[3072,64]{0,1:T(8,128)(2,1)S(1)}, bf16[3072,64]{0,1:T(8,128)(2,1)}, u32[]{:S(2)}) copy-start(bf16[3072,64]{0,1:T(8,128)(2,1)} %param.12) | copy-start | bytes 1179652
  0.6 8.5 %copy-start.3 = (bf16[1536,3072]{1,0:T(8,128)(2,1)S(1)}, bf16[1536,3072]{1,0:T(8,128)(2,1)}, u32[]{:S(2)}) copy-start(bf16[1536,3072]{1,0:T(8,128)(2,1)} %param.10) | copy-start | bytes 28311556
  9.1 14.9 %copy-start.5 = (s32[24]{0:T(128)S(1)}, s32[24]{0:T(128)}, u32[]{:S(2)}) copy-start(s32[24]{0:T(128)} %param.15) | copy-start | bytes 292
  26.4 17.9 %all-to-all-start = ((bf16[32,2,2048]{2,1,0:T(2,128)(2,1)}), bf16[32,2,2048]{2,1,0:T(2,128)(2,1)S(1)}, u32[]{:S(2)}, u32[]{:S(2)}) async-start(bf16[32,2,2048]{2,1,0:T(2,128)(2,1)} %reshape.100), calls=%async_computation | async-start | bytes 524288 | tf_op jit(solution)/shard_map/all_to_all | solution.py:101
  33.7 20.6 %copy-start.6 = (f32[512]{0:T(512)S(1)}, f32[512]{0:T(512)}, u32[]{:S(2)}) copy-start(f32[512]{0:T(512)} %param.17) | copy-start | bytes 6148
  46.6 5.8 %collective-permute-start = (bf16[2,2048]{1,0:T(2,128)(2,1)S(1)}, bf16[2,2048]{1,0:T(2,128)(2,1)S(1)}, u32[]{:S(2)}, u32[]{:S(2)}) collective-permute-start(bf16[2,2048]{1,0:T(2,128)(2,1)S(1)} %slice.109), channel_id=1, source_target_pairs={{0,1},{1,2},{2,3},{3,4},{4,5},{5,6},{6,7},{7,8},{8,9},{9,10},{10,1... | collective-permute-start | bytes 24584 | tf_op jit(solution)/shard_map/ppermute | solution.py:23
  48.6 4.0 %collective-permute-start.1 = (bf16[2,2048]{1,0:T(2,128)(2,1)S(1)}, bf16[2,2048]{1,0:T(2,128)(2,1)S(1)}, u32[]{:S(2)}, u32[]{:S(2)}) collective-permute-start(bf16[2,2048]{1,0:T(2,128)(2,1)S(1)} %slice.111), channel_id=1, source_target_pairs={{1,0},{2,1},{3,2},{4,3},{5,4},{6,5},{7,6},{8,7},{9,8},{10,9},{11,1... | collective-permute-start | bytes 24584 | tf_op jit(solution)/shard_map/ppermute | solution.py:24
  53.7 6.0 %slice-start = ((s8[4718592]{0:T(1024)(128)(4,1)}), s8[4194304]{0:T(1024)(128)(4,1)S(1)}, s32[]{:S(2)}) async-start(s8[4718592]{0:T(1024)(128)(4,1)} %bitcast.64), calls=%async_computation.1 | async-start | bytes 8388608
  54.3 5.4 %slice-start.1 = ((s8[4718592]{0:T(1024)(128)(4,1)}), s8[524288]{0:T(1024)(128)(4,1)S(1)}, s32[]{:S(2)}) async-start(s8[4718592]{0:T(1024)(128)(4,1)} %bitcast.64), calls=%async_computation.2 | async-start | bytes 1048576
  59.7 44.9 %copy-start.2 = (bf16[50,512,128]{1,2,0:T(8,128)(2,1)}, bf16[50,512,128]{1,2,0:T(8,128)(2,1)S(1)}, u32[]{:S(2)}) copy-start(bf16[50,512,128]{1,2,0:T(8,128)(2,1)S(1)} %get-tuple-element.18) | copy-start | bytes 19660804
  114.4 8.6 %copy-start.4 = (f32[512]{0:T(512)S(1)}, f32[512]{0:T(512)}, u32[]{:S(2)}) copy-start(f32[512]{0:T(512)} %param.19) | copy-start | bytes 6148
  123.0 45.3 %copy-start.1 = (bf16[3072,64]{0,1:T(8,128)(2,1)S(1)}, bf16[3072,64]{0,1:T(8,128)(2,1)}, u32[]{:S(2)}) copy-start(bf16[3072,64]{0,1:T(8,128)(2,1)} %param.12) | copy-start | bytes 1179652
where the time goes:
time: 171 us; the launch traced here: 168 us
  matrix products  108 us (63%)
  local copies, waits for them, and re-layouts  27.7 us (16%)
  starting transfers between devices  10.6 us (6%)
  waiting for transfers between devices  10.5 us (6%)
  other arithmetic  9.59 us (6%)
  between operations  1.83 us (1%)
    dot_general x9, matrix products, conv_three(): jnp.einsum('rkw,ko->row', window, weights[3 * row_off + col_off], preferr...  87.9 us
    unnamed x25, local copies, waits for them, and re-layouts  18.7 us
    dot_general x1, matrix products, shards(): partial_proj = jnp.dot(normed, weight_f, precision=lax.Precision.HIGHEST)  14.3 us
    all_to_all x1, waiting for transfers between devices, shards(): lax.all_to_all(sendbuf, 'wide', split_axis=0, concat_axis=0, tiled=True)  10.5 us
    all_to_all x1, starting transfers between devices, shards(): lax.all_to_all(sendbuf, 'wide', split_axis=0, concat_axis=0, tiled=True)  7.3 us
    reduce_sum x1, other arithmetic, shards(): jnp.sum(feats, axis=-1)  6.74 us
    dot_general x1, matrix products, conv_input_rows(): jnp.einsum('rwk,ko->rwo', patches, weight, preferred_element_type=jnp.flo...  5.32 us
    slice x1, local copies, waits for them, and re-layouts, shards(): decoder_features = features[depth - 1:depth - 1 + slab_height]  3.43 us
  transfers between devices with their start and end apart: 3, of which 1 were waited for; matrix products, arithmetic and copies ran while one was open for 2% of the time, Pallas kernels for 0%

commit v1 on v0

--- a/solution.py
+++ b/solution.py
@@ -1,19 +1,234 @@
+import functools
+
 import jax
 import jax.numpy as jnp
 from jax import lax
+from jax.experimental import pallas as pl
+from jax.experimental.pallas import tpu as pltpu
 from jax.sharding import PartitionSpec as P
 
 D = 3072
 LC = 16
 GRID = 64
 STEPS = 28
-
+WPIX = 2 * GRID
+PAIRS = 8
 
 shift_value = 3.0
 norm_eps = 1e-06
-
-
-def padded_2(value, sides, width):
+f32 = jnp.float32
+bf16 = jnp.bfloat16
+TRANS_B = (((1,), (1,)), ((), ()))
+
+
+def split3(x):
+    hi = x.astype(bf16)
+    rest = x - hi.astype(f32)
+    mid = rest.astype(bf16)
+    return hi, mid, (rest - mid.astype(f32)).astype(bf16)
+
+
+def project_kernel(features, sigma_ref, mod_ref, wt_ref, hidden_ref, noisy_ref, out_ref, wcat, consts):
+    values = wt_ref.shape[0]
+
+    @pl.when(pl.program_id(0) == 0)
+    def _():
+        wt = wt_ref[...]
+        parts = split3(wt.astype(f32) * (1.0 + mod_ref[1:2, :]))
+        for i, part in enumerate(parts):
+            wcat[i * values : (i + 1) * values, :] = part
+        wcat[3 * values :, :] = jnp.ones((values, wt.shape[1]), bf16)
+        ones = jnp.ones((16, wt.shape[1]), bf16)
+        sums = lax.dot_general(ones, wcat[...], TRANS_B, preferred_element_type=f32)
+        total = sums[:, :values] + sums[:, values : 2 * values] + sums[:, 2 * values : 3 * values]
+        shift = jnp.zeros((16, values), f32)
+        for part in split3(jnp.broadcast_to(mod_ref[0:1, :], (16, wt.shape[1]))):
+            shift = shift + lax.dot_general(part, wt, TRANS_B, preferred_element_type=f32)
+        consts[0:1, :] = total[0:1, :]
+        consts[1:2, :] = shift[0:1, :]
+
+    h = hidden_ref[...]
+    acc = lax.dot_general(h, wcat[...], TRANS_B, preferred_element_type=f32)
+    hf = h.astype(f32)
+    square = jnp.sum(hf * hf, axis=-1, keepdims=True)
+    hw = acc[:, :values] + acc[:, values : 2 * values] + acc[:, 2 * values : 3 * values]
+    mean = acc[:, 3 * values : 3 * values + 1] / features
+    rstd = 1.0 / jnp.sqrt(square / features - mean * mean + norm_eps)
+    velocity = rstd * (hw - mean * consts[0:1, :]) + consts[1:2, :]
+    out_ref[...] = (noisy_ref[...] - sigma_ref[0:1, :] * velocity).astype(bf16)
+
+
+def project(hidden, modulation, final_weight, noisy, sigma):
+    tokens, features = hidden.shape
+    values = final_weight.shape[1]
+    block = 256
+    return pl.pallas_call(
+        functools.partial(project_kernel, features),
+        grid=(tokens // block,),
+        in_specs=[
+            pl.BlockSpec((1, values), lambda i: (0, 0)),
+            pl.BlockSpec((2, features), lambda i: (0, 0)),
+            pl.BlockSpec((values, features), lambda i: (0, 0)),
+            pl.BlockSpec((block, features), lambda i: (i, 0)),
+            pl.BlockSpec((block, values), lambda i: (i, 0)),
+        ],
+        out_specs=pl.BlockSpec((block, values), lambda i: (i, 0)),
+        out_shape=jax.ShapeDtypeStruct((tokens, values), bf16),
+        scratch_shapes=[pltpu.VMEM((4 * values, features), bf16), pltpu.VMEM((8, values), f32)],
+        compiler_params=pltpu.CompilerParams(vmem_limit_bytes=40 << 20),
+        cost_estimate=pl.CostEstimate(flops=2 * tokens * features * 256, bytes_accessed=2 * tokens * features, transcendentals=0),
+        name="project",
+    )(jnp.broadcast_to(sigma, (1, values)), modulation, final_weight.T, hidden, noisy)
+
+
+def decode_kernel(pairs, mask_ref, patch_ref, win_ref, bin_ref, u_ref, b1_ref, feat_ref, res_ref, act, pad, tr):
+    step = pl.program_id(0)
+    width = WPIX
+    chans = win_ref.shape[1]
+    rows = 2 * pairs
+    chunk = 6
+
+    @pl.when(step == 0)
+    def _():
+        pad[:, 0:8, :] = jnp.zeros((chunk, 8, chans), f32)
+        pad[:, 8 + width :, :] = jnp.zeros((chunk, 8, chans), f32)
+
+    def first(c, carry):
+        base = pl.multiple_of((step * rows + c * chunk) * width, width)
+        x = patch_ref[pl.ds(base, chunk * width), :]
+        f = jnp.dot(x, win_ref[...], preferred_element_type=f32) + bin_ref[...]
+        for q in range(chunk):
+            fb = f[q * width : (q + 1) * width, :].astype(bf16)
+            row = c * chunk + q
+            fr = fb.astype(f32)
+
+            @pl.when((row >= 1) & (row <= rows))
+            def _():
+                feat_ref[row - 1] = fr.T.astype(bf16)
+
+            half = 0.5 * fr
+            a = half + half * jnp.tanh(half)
+            pad[q, 8 : 8 + width, :] = a
+            act[row, :, chans : 2 * chans] = a.astype(bf16)
+            act[row, :, 0:chans] = pad[q, 7 : 7 + width, :].astype(bf16)
+            act[row, :, 2 * chans :] = pad[q, 9 : 9 + width, :].astype(bf16)
+        return carry
+
+    lax.fori_loop(0, (rows + 2) // chunk, first, 0)
+
+    def transform(p, carry):
+        at = pl.ds(pl.multiple_of(p * width, width), width)
+        upper = mask_ref[0, step * pairs + p]
+        lower = mask_ref[1, step * pairs + p]
+        d1 = act[2 * p + 1]
+        d2 = act[2 * p + 2]
+        tr[1, at, :] = d1 + d2
+        tr[2, at, :] = d2 - d1
+        tr[0, at, :] = (act[2 * p].astype(f32) * upper - d2.astype(f32)).astype(bf16)
+        tr[3, at, :] = (d1.astype(f32) - act[2 * p + 3].astype(f32) * lower).astype(bf16)
+        return carry
+
+    lax.fori_loop(0, pairs, transform, 0)
+
+    tile = 256
+    for n in range(chans // tile):
+        cols = slice(n * tile, (n + 1) * tile)
+        bias = b1_ref[:, cols]
+        m = [jnp.dot(tr[k], u_ref[k, :, cols], preferred_element_type=f32) for k in range(4)]
+        y0 = m[0] + (m[1] + m[2]) + bias
+        y1 = (m[1] - m[2]) - m[3] + bias
+        for p in range(pairs):
+            at = slice(p * width, (p + 1) * width)
+            res_ref[2 * p, cols, :] = y0[at].T.astype(bf16)
+            res_ref[2 * p + 1, cols, :] = y1[at].T.astype(bf16)
+
+
+def decode(masks, patches, win, b_in, u, b1, height):
+    chans = win.shape[1]
+    rows = 2 * PAIRS
+    whole = lambda *shape: pl.BlockSpec(shape, lambda i: (0,) * len(shape), pipeline_mode=pl.Buffered(1))
+    shape = jax.ShapeDtypeStruct((height, chans, WPIX), bf16)
+    out = pl.BlockSpec((rows, chans, WPIX), lambda i: (i, 0, 0))
+    return pl.pallas_call(
+        functools.partial(decode_kernel, PAIRS),
+        grid=(height // rows,),
+        in_specs=[
+            pl.BlockSpec(memory_space=pltpu.SMEM),
+            whole(*patches.shape),
+            whole(*win.shape),
+            whole(1, chans),
+            whole(*u.shape),
+            whole(1, chans),
+        ],
+        out_specs=[out, out],
+        out_shape=[shape, shape],
+        scratch_shapes=[
+            pltpu.VMEM((rows + 2, WPIX, 3 * chans), bf16),
+            pltpu.VMEM((6, WPIX + 16, chans), f32),
+            pltpu.VMEM((4, PAIRS * WPIX, 3 * chans), bf16),
+        ],
+        compiler_params=pltpu.CompilerParams(vmem_limit_bytes=60 << 20),
+        cost_estimate=pl.CostEstimate(flops=height * WPIX * 12 * 512 * 512, bytes_accessed=30 << 20, transcendentals=0),
+        name="decode",
+    )(masks, patches, win, b_in[None], u, b1[None])
+
+
+def edge_masks(first_row, count, height):
+    global_rows = first_row + jnp.arange(count, dtype=jnp.int32)
+    upper = (global_rows % height != 0).astype(f32)
+    lower = (global_rows % height != height - 1).astype(f32)
+    return (upper, jnp.ones_like(upper), lower)
+
+
+def padded_2(value, axis, width):
+    count, length = (lax.axis_size(axis), value.shape[0])
+    up = [(i, (i + 1) % count) for i in range(count - 1)]
+    down = [(j, i) for i, j in up]
+    before = lax.ppermute(value[length - width :], axis, up)
+    after = lax.ppermute(value[:width], axis, down)
+    return jnp.concatenate([before, value, after], axis=0)
+
+
+def patches_of(latent, first_row, count):
+    planes = latent.reshape(latent.shape[0], WPIX, LC)
+    padded = jnp.pad(planes, ((0, 0), (1, 1), (0, 0)))
+    masks = edge_masks(first_row, count, WPIX)
+    pieces = []
+    for row_off in range(3):
+        keep = masks[row_off].astype(bf16)[:, None, None]
+        for col_off in range(3):
+            pieces.append(padded[row_off : row_off + count, col_off : col_off + WPIX, :] * keep)
+    return jnp.concatenate(pieces, axis=-1).reshape(count * WPIX, 9 * LC)
+
+
+def shards(hidden, modulation, final_weight, noisy, step_index, slab_table, conv_in_weight, conv_in_bias, conv1_weight, conv1_bias):
+    frac = step_index[0].astype(f32) / STEPS
+    sigma = shift_value * frac / (1.0 + (shift_value - 1.0) * frac)
+    clean = project(hidden, modulation, final_weight, noisy, sigma)
+    rows_here = slab_table.shape[0]
+    token_rows = clean.reshape(rows_here, -1)
+    slabs = lax.axis_size("wide")
+    slab_here = lax.axis_index("wide")
+    slab_ids = jnp.arange(slabs, dtype=jnp.int32)
+    outgoing = (slab_ids[:, None] == slab_table[None, :]).astype(bf16)
+    sendbuf = jnp.dot(outgoing, token_rows, preferred_element_type=f32).astype(bf16)
+    received = lax.all_to_all(sendbuf, "wide", split_axis=0, concat_axis=0, tiled=True)
+    g = conv1_weight.reshape(3, 3 * conv1_weight.shape[1], conv1_weight.shape[2])
+    gf = g.astype(f32)
+    u = jnp.stack([g[0], (0.5 * (gf[0] + gf[1] + gf[2])).astype(bf16), (0.5 * (gf[0] - gf[1] + gf[2])).astype(bf16), g[2]])
+    source = (2 * slab_here - slab_table) % slabs
+    incoming = (source[:, None] == slab_ids[None, :]).astype(bf16)
+    slab_rows = jnp.dot(incoming, received, preferred_element_type=f32).astype(bf16)
+    pixel_rows = slab_rows.reshape(rows_here, GRID, 2, 2, LC).transpose(0, 2, 1, 3, 4).reshape(2 * rows_here, WPIX * LC)
+    latent = padded_2(pixel_rows, "wide", 2)
+    height = 2 * rows_here
+    patches = patches_of(latent, slab_here * height - 1, height + 2)
+    tops = slab_here * height + 2 * jnp.arange(rows_here, dtype=jnp.int32)
+    masks = jnp.stack([tops % WPIX != 0, (tops + 2) % WPIX != 0]).astype(f32)
+    return tuple(decode(masks, patches, conv_in_weight, conv_in_bias, u, conv1_bias, height))
+
+
+def split_padded(value, sides, width):
     for axis, dim in sides:
         count, length = (lax.axis_size(axis), value.shape[dim])
         up = [(i, (i + 1) % count) for i in range(count - 1)]
@@ -24,13 +239,6 @@
         after = lax.ppermute(first, axis, down)
         value = jnp.concatenate([before, value, after], axis=dim)
     return value
-
-
-def edge_masks(first_row, count, height):
-    global_rows = first_row + jnp.arange(count, dtype=jnp.int32)
-    upper = (global_rows % height != 0).astype(jnp.float32)
-    lower = (global_rows % height != height - 1).astype(jnp.float32)
-    return (upper, jnp.ones_like(upper), lower)
 
 
 def conv_input_rows(latent, weight, bias, first_row, count, channels):
@@ -65,7 +273,7 @@
     return total
 
 
-def shards(
+def split_shards(
     hidden,
     modulation,
     final_weight,
@@ -110,7 +318,7 @@
         .reshape(2 * rows_here, 4 * grid_side * channels // 2)
     )
     depth = 2
-    latent = padded_2(pixel_rows, (("wide", 0),), depth)
+    latent = split_padded(pixel_rows, (("wide", 0),), depth)
     slab_height = 2 * rows_here
     conv_rows = slab_height + 2 * (depth - 1)
     first_conv = slab_here * slab_height - (depth - 1)
@@ -132,8 +340,9 @@
 
 
 def solution(mesh):
+    whole_channels = mesh.shape["tensor"] == 1
     return jax.shard_map(
-        shards,
+        shards if whole_channels else split_shards,
         mesh=mesh,
         in_specs=(
             P("wide", "tensor"),

time: 171 us -> 105 us (0.61)
  the two profiles are of different devices: /device:TPU:0 before, /device:TPU:7 now
where the time goes in v1:
time: 105 us
  Pallas kernels  52.6 us (50%)
  local copies, waits for them, and re-layouts  20.3 us (19%)
  other arithmetic  15.8 us (15%)
  starting transfers between devices  11.8 us (11%)
  waiting for transfers between devices  2.16 us (2%)
  between operations  1.6 us (2%)
    pallas_call x1, Pallas kernels, decode(): pl.pallas_call(functools.partial(decode_kernel, PAIRS), grid=(height // r...  46.9 us
    unnamed x16, local copies, waits for them, and re-layouts  9.17 us
    all_to_all x1, starting transfers between devices, shards(): lax.all_to_all(sendbuf, 'wide', split_axis=0, concat_axis=0, tiled=True)  6.39 us
    pallas_call x1, Pallas kernels, project(): pl.pallas_call(functools.partial(project_kernel, features), grid=(tokens...  5.77 us
    another operation x1, other arithmetic  5.05 us
    convert_element_type x1, other arithmetic, shards(): gf = g.astype(f32)  5 us
    concatenate x1, local copies, waits for them, and re-layouts, patches_of(): return jnp.concatenate(pieces, axis=-1).reshape(count * WPIX, 9 * LC)  3.71 us
    ppermute x1, starting transfers between devices, padded_2(): before = lax.ppermute(value[length - width:], axis, up)  3.33 us
  transfers between devices with their start and end apart: 3, of which 1 were waited for; matrix products, arithmetic and copies ran while one was open for 18% of the time, Pallas kernels for 0%

profile of v1, /device:TPU:7, one launch (start us, length us, event | category | flops | bytes accessed | tf_op | source)
XLA Modules:
  0.0 104.9 jit_solution(10708516651952438195)
XLA Ops:
  1.3 1.3 %copy.34.noisy_ref = f32[1536,64]{1,0:T(8,128)S(1)} copy(f32[1536,64]{0,1:T(8,128)} %param.13) | data formatting | bytes 786432 | tf_op args[3]
  2.6 0.0 copy-start
  2.6 3.7 %copy-done = bf16[1536,3072]{1,0:T(8,128)(2,1)S(1)} copy-done((bf16[1536,3072]{1,0:T(8,128)(2,1)S(1)}, bf16[1536,3072]{1,0:T(8,128)(2,1)}, u32[]{:S(2)}) %copy-start) | copy-done | bytes 9437208
  6.3 1.0 copy-done.1
  7.3 0.7 copy-done.2
  8.0 5.8 %project.1 = bf16[1536,64]{1,0:T(8,128)(2,1)S(1)} custom-call(f32[1,64]{1,0:T(1,128)S(1)} %broadcast_in_dim.6.sigma_ref, f32[2,3072]{1,0:T(2,128)S(1)} %copy-done.2, bf16[64,3072]{1,0:T(8,128)(2,1)S(1)} %bitcast.17, bf16[1536,3072]{1,0:T(8,128)(2,1)S(1)} %copy-done, f32[1536,64]{1,0:T(8,128)S(1)} %copy.34.noisy_ref), custom_call_target="tpu_custom_call" | custom-call | flops 2415919104 | bytes 9437184 | tf_op jit(solution)/shard_map/project/pallas_call | solution.py:65
  13.8 0.4 reshape.159
  14.2 0.0 copy-done.4
  14.2 0.2 fusion
  14.4 0.5 broadcast.214
  14.9 0.8 reduce
  15.7 0.9 reshape.162
  16.6 6.4 %all-to-all-start = ((bf16[32,2,2048]{2,1,0:T(2,128)(2,1)}), bf16[32,2,2048]{2,1,0:T(2,128)(2,1)S(1)}, u32[]{:S(2)}, u32[]{:S(2)}) async-start(bf16[32,2,2048]{2,1,0:T(2,128)(2,1)} %reshape.162), calls=%async_computation | async-start | bytes 524288 | tf_op jit(solution)/shard_map/all_to_all | solution.py:215
  23.0 0.0 copy-start.3
  23.0 2.2 %fusion.25 = (bf16[3,512,512]{2,1,0:T(8,128)(2,1)S(1)}, bf16[3,512,512]{2,1,0:T(8,128)(2,1)S(1)}) fusion(bf16[9,512,512]{2,1,0:T(8,128)(2,1)} %param.18), kind=kLoop, calls=%fused_computation.58 | loop fusion | bytes 6291456 | tf_op jit(solution)/shard_map/slice | solution.py:218
  25.3 1.0 copy-done.3
  26.3 5.0 %convert_element_type.61 = f32[9,512,512]{2,1,0:T(8,128)} convert(bf16[9,512,512]{2,1,0:T(8,128)(2,1)S(1)} %copy-done.3) | non-fusion elementwise | flops 2359296 | bytes 14155776 | tf_op jit(solution)/shard_map/convert_element_type | solution.py:217
  31.3 5.0 %multiply_convert_fusion.1 = (bf16[3,512,512]{2,1,0:T(8,128)(2,1)S(1)}, bf16[3,512,512]{2,1,0:T(8,128)(2,1)S(1)}) fusion(f32[9,512,512]{2,1,0:T(8,128)} %convert_element_type.61), kind=kLoop, calls=%fused_computation.5 | loop fusion | flops 6291456 | bytes 12582912 | tf_op jit(solution)/shard_map/convert.1
  36.4 0.5 add_convert_fusion.mask_ref
  36.9 3.2 %pad_maximum_fusion.u_ref = bf16[4,1536,512]{2,1,0:T(8,128)(2,1)} fusion(bf16[1,1536,512]{2,1,0:T(8,128)(2,1)S(1)} %bitcast.23, bf16[1,1536,512]{2,1,0:T(8,128)(2,1)S(1)} %bitcast.21, bf16[1,1536,512]{2,1,0:T(8,128)(2,1)S(1)} %bitcast.20, bf16[1,1536,512]{2,1,0:T(8,128)(2,1)S(1)} %bitcast.22), kind=kLoop, calls=%fused_computation | loop fusion | flops 9437184 | bytes 12582912 | tf_op jit(solution)/shard_map/stack | solution.py:218
  40.1 0.0 all-to-all-done
  40.1 0.3 reshape.163
  40.4 0.4 convolution_convert_fusion.1
  40.8 1.3 %reshape.160 = bf16[24,64,2,2,16]{4,3,2,1,0:T(2,128)(2,1)S(1)} reshape(bf16[24,4096]{1,0:T(8,128)(2,1)S(1)} %convolution_convert_fusion.1) | data formatting | bytes 393216 | tf_op jit(solution)/shard_map/reshape | solution.py:222
  42.1 0.1 fusion.26
  42.2 0.1 slice.68
  42.4 3.3 %collective-permute-start = (bf16[2,2048]{1,0:T(2,128)(2,1)S(1)}, bf16[2,2048]{1,0:T(2,128)(2,1)S(1)}, u32[]{:S(2)}, u32[]{:S(2)}) collective-permute-start(bf16[2,2048]{1,0:T(2,128)(2,1)S(1)} %slice.68), channel_id=1, source_target_pairs={{0,1},{1,2},{2,3},{3,4},{4,5},{5,6},{6,7},{7,8},{8,9},{9,10},{10,1... | collective-permute-start | bytes 24584 | tf_op jit(solution)/shard_map/ppermute | solution.py:187
  45.7 0.1 slice.70
  45.9 2.1 %collective-permute-start.1 = (bf16[2,2048]{1,0:T(2,128)(2,1)S(1)}, bf16[2,2048]{1,0:T(2,128)(2,1)S(1)}, u32[]{:S(2)}, u32[]{:S(2)}) collective-permute-start(bf16[2,2048]{1,0:T(2,128)(2,1)S(1)} %slice.70), channel_id=1, source_target_pairs={{1,0},{2,1},{3,2},{4,3},{5,4},{6,5},{7,6},{8,7},{9,8},{10,9},{11,1... | collective-permute-start | bytes 24584 | tf_op jit(solution)/shard_map/ppermute | solution.py:188
  48.0 1.7 %copy.37 = bf16[24,2,64,2,16]{4,3,2,1,0:T(2,128)(2,1)S(1)} copy(bf16[24,2,64,2,16]{4,3,1,2,0:T(2,128)(2,1)S(1)} %bitcast.19) | data formatting | bytes 393216 | tf_op jit(solution)/shard_map/transpose | solution.py:222
  49.7 0.6 copy.40
  50.3 0.0 collective-permute-done
  50.3 0.1 concatenate.19
  50.4 0.1 copy.39
  50.5 2.2 %collective-permute-done.1 = bf16[2,2048]{1,0:T(2,128)(2,1)S(1)} collective-permute-done((bf16[2,2048]{1,0:T(2,128)(2,1)S(1)}, bf16[2,2048]{1,0:T(2,128)(2,1)S(1)}, u32[]{:S(2)}, u32[]{:S(2)}) %collective-permute-start.1) | collective-permute-done | bytes 8224 | tf_op jit(solution)/shard_map/ppermute | solution.py:188
  52.6 0.1 concatenate.21
  52.7 0.1 copy.41
  52.8 0.1 pad_maximum_fusion.1
  52.9 0.2 fusion.4
  53.1 0.1 fusion.13
  53.2 0.2 fusion.6
  53.4 0.1 fusion.7
  53.6 0.1 fusion.8
  53.8 0.2 fusion.10
  54.0 0.1 fusion.14
  54.1 0.2 fusion.12
  54.4 3.7 %copy.46 = bf16[50,128,144]{2,1,0:T(8,128)(2,1)} copy(bf16[50,128,144]{1,2,0:T(8,128)(2,1)S(1)} %fusion.12) | data formatting | bytes 3686400 | tf_op jit(solution)/shard_map/concatenate | solution.py:201
  58.1 46.9 %decode.1 = (bf16[48,512,128]{2,1,0:T(8,128)(2,1)}, bf16[48,512,128]{2,1,0:T(8,128)(2,1)}) custom-call(f32[2,24]{1,0:T(2,128)} %add_convert_fusion.mask_ref, bf16[6400,144]{1,0:T(8,128)(2,1)} %bitcast.25, bf16[144,512]{1,0:T(8,128)(2,1)} %win_ref.1, f32[1,512]{1,0:T(1,128)} %bitcast.26, bf16[4,1536,512]{2,1,0:T(8,128)(2,1)} %pad_maximum_fusion.u_ref, ...), custom_call_target="tpu_custom_call" | custom-call | flops 19327352832 | bytes 31457280 | tf_op jit(solution)/shard_map/decode/pallas_call | solution.py:152
  (11 shorter events, 0.2 us)
Async XLA Ops:
  2.6 3.7 %copy-start = (bf16[1536,3072]{1,0:T(8,128)(2,1)S(1)}, bf16[1536,3072]{1,0:T(8,128)(2,1)}, u32[]{:S(2)}) copy-start(bf16[1536,3072]{1,0:T(8,128)(2,1)} %hidden_ref.1) | copy-start | bytes 28311556
  6.3 1.0 copy-start.1
  7.3 0.7 copy-start.2
  8.0 6.1 %copy-start.4 = (s32[24]{0:T(128)S(1)}, s32[24]{0:T(128)}, u32[]{:S(2)}) copy-start(s32[24]{0:T(128)} %param.15) | copy-start | bytes 292
  16.6 23.5 %all-to-all-start = ((bf16[32,2,2048]{2,1,0:T(2,128)(2,1)}), bf16[32,2,2048]{2,1,0:T(2,128)(2,1)S(1)}, u32[]{:S(2)}, u32[]{:S(2)}) async-start(bf16[32,2,2048]{2,1,0:T(2,128)(2,1)} %reshape.162), calls=%async_computation | async-start | bytes 524288 | tf_op jit(solution)/shard_map/all_to_all | solution.py:215
  23.0 3.3 %copy-start.3 = (bf16[9,512,512]{2,1,0:T(8,128)(2,1)S(1)}, bf16[9,512,512]{2,1,0:T(8,128)(2,1)}, u32[]{:S(2)}) copy-start(bf16[9,512,512]{2,1,0:T(8,128)(2,1)} %param.18) | copy-start | bytes 14155780
  42.4 7.9 %collective-permute-start = (bf16[2,2048]{1,0:T(2,128)(2,1)S(1)}, bf16[2,2048]{1,0:T(2,128)(2,1)S(1)}, u32[]{:S(2)}, u32[]{:S(2)}) collective-permute-start(bf16[2,2048]{1,0:T(2,128)(2,1)S(1)} %slice.68), channel_id=1, source_target_pairs={{0,1},{1,2},{2,3},{3,4},{4,5},{5,6},{6,7},{7,8},{8,9},{9,10},{10,1... | collective-permute-start | bytes 24584 | tf_op jit(solution)/shard_map/ppermute | solution.py:187
  45.9 6.8 %collective-permute-start.1 = (bf16[2,2048]{1,0:T(2,128)(2,1)S(1)}, bf16[2,2048]{1,0:T(2,128)(2,1)S(1)}, u32[]{:S(2)}, u32[]{:S(2)}) collective-permute-start(bf16[2,2048]{1,0:T(2,128)(2,1)S(1)} %slice.70), channel_id=1, source_target_pairs={{1,0},{2,1},{3,2},{4,3},{5,4},{6,5},{7,6},{8,7},{9,8},{10,9},{11,1... | collective-permute-start | bytes 24584 | tf_op jit(solution)/shard_map/ppermute | solution.py:188

commit v2 on v0

--- a/solution.py
+++ b/solution.py
@@ -1,19 +1,369 @@
+import functools
+
 import jax
 import jax.numpy as jnp
+import numpy as np
 from jax import lax
+from jax.experimental import pallas as pl
+from jax.experimental.pallas import tpu as pltpu
 from jax.sharding import PartitionSpec as P
 
 D = 3072
 LC = 16
 GRID = 64
 STEPS = 28
-
+WPIX = 2 * GRID
+HALF = GRID // 2
+CHUNK = 4
+MESH = pl.DeviceIdType.MESH
 
 shift_value = 3.0
 norm_eps = 1e-06
-
-
-def padded_2(value, sides, width):
+f32 = jnp.float32
+bf16 = jnp.bfloat16
+TRANS_B = (((1,), (1,)), ((), ()))
+
+
+def split3(x):
+    hi = x.astype(bf16)
+    rest = x - hi.astype(f32)
+    mid = rest.astype(bf16)
+    return hi, mid, (rest - mid.astype(f32)).astype(bf16)
+
+
+def relay_kernel(slabs, features, inv_ref, src_ref, sigma_ref, mod_ref, wt_ref, hidden_ref, noisy_ref, x_ref, wcat, consts, rows, sendbuf, recv, ordered, halo, shifted, wide, send_sem, recv_sem, edge_send, edge_recv):
+    step = pl.program_id(0)
+    me = lax.axis_index("wide")
+    values = wt_ref.shape[0]
+    count = rows.shape[0]
+    barrier = pltpu.get_barrier_semaphore()
+
+    @pl.when(step == 0)
+    def _():
+        for k in range(1, slabs):
+            pl.semaphore_signal(barrier, inc=1, device_id={"wide": lax.rem(me + k, slabs)}, device_id_type=MESH)
+        wt = wt_ref[...]
+        parts = split3(wt.astype(f32) * (1.0 + mod_ref[1:2, :]))
+        for i, part in enumerate(parts):
+            wcat[i * values : (i + 1) * values, :] = part
+        wcat[3 * values :, :] = jnp.ones((values, wt.shape[1]), bf16)
+        ones = jnp.ones((16, wt.shape[1]), bf16)
+        sums = lax.dot_general(ones, wcat[...], TRANS_B, preferred_element_type=f32)
+        total = sums[:, :values] + sums[:, values : 2 * values] + sums[:, 2 * values : 3 * values]
+        shift = jnp.zeros((16, values), f32)
+        for part in split3(jnp.broadcast_to(mod_ref[0:1, :], (16, wt.shape[1]))):
+            shift = shift + lax.dot_general(part, wt, TRANS_B, preferred_element_type=f32)
+        consts[0:1, :] = total[0:1, :]
+        consts[1:2, :] = shift[0:1, :]
+
+    h = hidden_ref[...]
+    acc = lax.dot_general(h, wcat[...], TRANS_B, preferred_element_type=f32)
+    hf = h.astype(f32)
+    square = jnp.sum(hf * hf, axis=-1, keepdims=True)
+    hw = acc[:, :values] + acc[:, values : 2 * values] + acc[:, 2 * values : 3 * values]
+    mean = acc[:, 3 * values : 3 * values + 1] / features
+    rstd = 1.0 / jnp.sqrt(square / features - mean * mean + norm_eps)
+    velocity = rstd * (hw - mean * consts[0:1, :]) + consts[1:2, :]
+    clean = noisy_ref[...] - sigma_ref[0:1, :] * velocity
+    here = h.shape[0] // GRID
+    for t in range(here):
+        pair = [clean[t * GRID : t * GRID + HALF], clean[t * GRID + HALF : (t + 1) * GRID]]
+        rows[step * here + t] = jnp.concatenate(pair, axis=1).astype(bf16)
+
+    @pl.when(step == pl.num_programs(0) - 1)
+    def _():
+        pl.semaphore_wait(barrier, slabs - 1)
+        for d in range(slabs):
+            sendbuf[d] = rows[inv_ref[d]]
+        copies = []
+        for k in range(1, slabs):
+            peer = lax.rem(me + k, slabs)
+            copy = pltpu.make_async_remote_copy(
+                src_ref=sendbuf.at[peer],
+                dst_ref=recv.at[me],
+                send_sem=send_sem.at[k],
+                recv_sem=recv_sem.at[k],
+                device_id={"wide": peer},
+                device_id_type=MESH,
+            )
+            copy.start()
+            copies.append(copy)
+        recv[me] = sendbuf[me]
+        for copy in copies:
+            copy.wait_recv()
+        for j in range(count):
+            ordered[j] = recv[src_ref[j]]
+        edges = []
+        for e, (row, peer) in enumerate(((count - 1, lax.rem(me + 1, slabs)), (0, lax.rem(me + slabs - 1, slabs)))):
+            copy = pltpu.make_async_remote_copy(
+                src_ref=ordered.at[row],
+                dst_ref=halo.at[e],
+                send_sem=edge_send.at[e],
+                recv_sem=edge_recv.at[e],
+                device_id={"wide": peer},
+                device_id_type=MESH,
+            )
+            copy.start()
+            edges.append(copy)
+
+        lane = lax.broadcasted_iota(jnp.int32, (GRID, 2 * GRID), 1)
+        own = lane < GRID
+        from_left = (lane // LC) % 2 == 1
+        from_upper = (lane // (2 * LC)) % 2 == 1
+        zeros = jnp.zeros((8, 2 * GRID), f32)
+
+        def widen(packed, at):
+            p = packed.astype(f32)
+            swapped = jnp.concatenate([p[:, GRID:], p[:, :GRID]], axis=1)
+            twice = jnp.concatenate([jnp.where(own[:HALF], p, swapped), jnp.where(own[:HALF], swapped, p)], axis=0)
+            shifted[at, 0:8, :] = zeros
+            shifted[at, 8 : 8 + GRID, :] = twice
+            shifted[at, 8 + GRID :, :] = zeros
+            beside = jnp.where(from_left, shifted[at, 7 : 7 + GRID, :], shifted[at, 9 : 9 + GRID, :])
+            wide[at] = jnp.where(own, twice, beside)
+
+        for j in range(count):
+            widen(ordered[j], j + 1)
+        for copy in edges:
+            copy.wait_recv()
+        widen(halo[0], 0)
+        widen(halo[1], count + 1)
+        for i in range(count + 2):
+            first = me * count + i - 1 + GRID
+            upper = jnp.where(lax.rem(first, GRID) != 0, 1.0, 0.0).astype(f32)
+            lower = jnp.where(lax.rem(first + 1, GRID) != 0, 1.0, 0.0).astype(f32)
+            above = wide[max(i - 1, 0)] * upper
+            below = wide[min(i + 1, count + 1)] * lower
+            x_ref[i * GRID : (i + 1) * GRID, 0 : 2 * GRID] = wide[i].astype(bf16)
+            x_ref[i * GRID : (i + 1) * GRID, 2 * GRID :] = jnp.where(from_upper, above, below).astype(bf16)
+        for copy in copies + edges:
+            copy.wait_send()
+
+
+def relay(hidden, modulation, final_weight, noisy, sigma, inverse, source, slabs):
+    tokens, features = hidden.shape
+    values = final_weight.shape[1]
+    count = source.shape[0]
+    block = 256
+    smem = pl.BlockSpec(memory_space=pltpu.SMEM)
+    row = (HALF, 2 * values)
+    return pl.pallas_call(
+        functools.partial(relay_kernel, slabs, features),
+        grid=(tokens // block,),
+        in_specs=[
+            smem,
+            smem,
+            pl.BlockSpec((1, values), lambda i: (0, 0)),
+            pl.BlockSpec((2, features), lambda i: (0, 0)),
+            pl.BlockSpec((values, features), lambda i: (0, 0)),
+            pl.BlockSpec((block, features), lambda i: (i, 0)),
+            pl.BlockSpec((block, values), lambda i: (i, 0)),
+        ],
+        out_specs=pl.BlockSpec(((count + 2) * GRID, 4 * values), lambda i: (0, 0)),
+        out_shape=jax.ShapeDtypeStruct(((count + 2) * GRID, 4 * values), bf16),
+        scratch_shapes=[
+            pltpu.VMEM((4 * values, features), bf16),
+            pltpu.VMEM((8, values), f32),
+            pltpu.VMEM((count,) + row, bf16),
+            pltpu.VMEM((slabs,) + row, bf16),
+            pltpu.VMEM((slabs,) + row, bf16),
+            pltpu.VMEM((count,) + row, bf16),
+            pltpu.VMEM((2,) + row, bf16),
+            pltpu.VMEM((count + 2, GRID + 16, 2 * values), f32),
+            pltpu.VMEM((count + 2, GRID, 2 * values), f32),
+            pltpu.SemaphoreType.DMA((slabs,)),
+            pltpu.SemaphoreType.DMA((slabs,)),
+            pltpu.SemaphoreType.DMA((2,)),
+            pltpu.SemaphoreType.DMA((2,)),
+        ],
+        compiler_params=pltpu.CompilerParams(vmem_limit_bytes=40 << 20, collective_id=0, has_side_effects=True),
+        cost_estimate=pl.CostEstimate(flops=2 * tokens * features * 256, bytes_accessed=2 * tokens * features, transcendentals=0),
+        name="relay",
+    )(inverse, source, jnp.broadcast_to(sigma, (1, values)), modulation, final_weight.T, hidden, noisy)
+
+
+def spread_table():
+    table = np.zeros((4, 4 * GRID, 9 * LC), np.float32)
+    for at in range(4 * GRID):
+        lane = at % (2 * GRID)
+        a, b, c = (lane // (2 * LC)) % 2, (lane // LC) % 2, lane % LC
+        row = a if at < 2 * GRID else (a - 2 if a == 1 else a + 2)
+        col = b if lane < GRID else (b - 2 if b == 1 else b + 2)
+        for pixel in range(4):
+            dr, dc = row - pixel // 2 + 1, col - pixel % 2 + 1
+            if 0 <= dr < 3 and 0 <= dc < 3:
+                table[pixel, at, (3 * dr + dc) * LC + c] = 1.0
+    return table.reshape(-1, 9 * LC)
+
+
+def decode_kernel(mask_ref, x_ref, spread_ref, win_ref, bin_ref, g_ref, b1_ref, feat_ref, res_ref, wbig, mixed, nat, pad, act, tr_a, tr_b):
+    step = pl.program_id(0)
+    last = pl.num_programs(0) - 1
+    chans = win_ref.shape[1]
+    patch = x_ref.shape[1]
+    pixel_rows = 2 * CHUNK
+    tile = 256
+
+    def setup():
+        pad[:, 0:8, :] = jnp.zeros((pixel_rows + 2, 8, chans), f32)
+        pad[:, 8 + WPIX :, :] = jnp.zeros((pixel_rows + 2, 8, chans), f32)
+        for pixel in range(4):
+            part = spread_ref[pixel * patch : (pixel + 1) * patch, :]
+            wbig[pixel] = jnp.dot(part, win_ref[...], preferred_element_type=f32).astype(bf16)
+
+        def mix(i, carry):
+            at = pl.ds(pl.multiple_of(i * 64, 64), 64)
+            outer = 0.5 * (g_ref[0, at, :].astype(f32) + g_ref[2, at, :].astype(f32))
+            inner = 0.5 * g_ref[1, at, :].astype(f32)
+            mixed[0, at, :] = (outer + inner).astype(bf16)
+            mixed[1, at, :] = (outer - inner).astype(bf16)
+            return carry
+
+        lax.fori_loop(0, g_ref.shape[1] // 64, mix, 0)
+
+    def prepare(tr):
+        base = step * CHUNK * GRID
+
+        def first(start, length, pixel):
+            x = x_ref[pl.ds(pl.multiple_of(start, GRID), length), :]
+            f = jnp.dot(x, wbig[pixel], preferred_element_type=f32) + bin_ref[...]
+            return f.astype(bf16).astype(f32)
+
+        def keep(f, row, b):
+            for c in range(chans // 128):
+                nat[row, c, pl.ds(b, GRID, stride=2), :] = f[:, c * 128 : (c + 1) * 128]
+
+        for b in range(2):
+            keep(first(base, GRID, 2 + b), 0, b)
+            keep(first(base + (CHUNK + 1) * GRID, GRID, b), pixel_rows + 1, b)
+        for pixel in range(4):
+            f = first(base + GRID, CHUNK * GRID, pixel)
+            for t in range(CHUNK):
+                keep(f[t * GRID : (t + 1) * GRID], 1 + 2 * t + pixel // 2, pixel % 2)
+        for r in range(pixel_rows + 2):
+            f = jnp.concatenate([nat[r, c] for c in range(chans // 128)], axis=1)
+            if 1 <= r <= pixel_rows:
+                feat_ref[r - 1] = f.astype(bf16).T
+            half = 0.5 * f
+            a = half + half * jnp.tanh(half)
+            if r == 0:
+                a = a * mask_ref[0, step]
+            if r == pixel_rows + 1:
+                a = a * mask_ref[1, step]
+            pad[r, 8 : 8 + WPIX, :] = a
+            act[r, :, chans : 2 * chans] = a.astype(bf16)
+            act[r, :, 0:chans] = pad[r, 7 : 7 + WPIX, :].astype(bf16)
+            act[r, :, 2 * chans :] = pad[r, 9 : 9 + WPIX, :].astype(bf16)
+        for p in range(CHUNK):
+            at = slice(p * WPIX, (p + 1) * WPIX)
+            d = [act[2 * p + i] for i in range(4)]
+            tr[0, at, :] = d[0] - d[2]
+            tr[1, at, :] = d[1] + d[2]
+            tr[2, at, :] = d[2] - d[1]
+            tr[3, at, :] = d[1] - d[3]
+
+    def residual(tr):
+        for n in range(chans // tile):
+            cols = slice(n * tile, (n + 1) * tile)
+            bias = b1_ref[:, cols]
+            factors = (g_ref[0, :, cols], mixed[0, :, cols], mixed[1, :, cols], g_ref[2, :, cols])
+            m = [jnp.dot(tr[k], factors[k], preferred_element_type=f32) for k in range(4)]
+            y0 = m[0] + (m[1] + m[2]) + bias
+            y1 = (m[1] - m[2]) - m[3] + bias
+            for p in range(CHUNK):
+                at = slice(p * WPIX, (p + 1) * WPIX)
+                res_ref[2 * p, cols, :] = y0[at].astype(bf16).T
+                res_ref[2 * p + 1, cols, :] = y1[at].astype(bf16).T
+
+    @pl.when(step == 0)
+    def _():
+        setup()
+        prepare(tr_a)
+
+    @pl.when((step > 0) & (step < last) & (lax.rem(step, 2) == 1))
+    def _():
+        residual(tr_a)
+        prepare(tr_b)
+
+    @pl.when((step > 0) & (step < last) & (lax.rem(step, 2) == 0))
+    def _():
+        residual(tr_b)
+        prepare(tr_a)
+
+    @pl.when((step == last) & (lax.rem(step, 2) == 1))
+    def _():
+        residual(tr_a)
+
+    @pl.when((step == last) & (lax.rem(step, 2) == 0))
+    def _():
+        residual(tr_b)
+
+
+def decode(masks, x, win, b_in, g, b1, height):
+    chans = win.shape[1]
+    rows = 2 * CHUNK
+    steps = height // rows
+    whole = lambda *shape: pl.BlockSpec(shape, lambda i: (0,) * len(shape), pipeline_mode=pl.Buffered(1))
+    shape = jax.ShapeDtypeStruct((height, chans, WPIX), bf16)
+    spread = jnp.asarray(spread_table(), bf16)
+    return pl.pallas_call(
+        decode_kernel,
+        grid=(steps + 1,),
+        in_specs=[
+            pl.BlockSpec(memory_space=pltpu.SMEM),
+            whole(*x.shape),
+            whole(*spread.shape),
+            whole(*win.shape),
+            whole(1, chans),
+            whole(*g.shape),
+            whole(1, chans),
+        ],
+        out_specs=[
+            pl.BlockSpec((rows, chans, WPIX), lambda i: (jnp.minimum(i, steps - 1), 0, 0)),
+            pl.BlockSpec((rows, chans, WPIX), lambda i: (jnp.maximum(i - 1, 0), 0, 0)),
+        ],
+        out_shape=[shape, shape],
+        scratch_shapes=[
+            pltpu.VMEM((4, x.shape[1], chans), bf16),
+            pltpu.VMEM((2,) + g.shape[1:], bf16),
+            pltpu.VMEM((rows + 2, chans // 128, WPIX, 128), f32),
+            pltpu.VMEM((rows + 2, WPIX + 16, chans), f32),
+            pltpu.VMEM((rows + 2, WPIX, 3 * chans), bf16),
+            pltpu.VMEM((4, CHUNK * WPIX, 3 * chans), bf16),
+            pltpu.VMEM((4, CHUNK * WPIX, 3 * chans), bf16),
+        ],
+        compiler_params=pltpu.CompilerParams(vmem_limit_bytes=60 << 20),
+        cost_estimate=pl.CostEstimate(flops=height * WPIX * 12 * 512 * 512, bytes_accessed=30 << 20, transcendentals=0),
+        name="decode",
+    )(masks, x, spread, win, b_in[None], g, b1[None])
+
+
+def shards(hidden, modulation, final_weight, noisy, step_index, slab_table, conv_in_weight, conv_in_bias, conv1_weight, conv1_bias):
+    frac = step_index[0].astype(f32) / STEPS
+    sigma = shift_value * frac / (1.0 + (shift_value - 1.0) * frac)
+    rows_here = slab_table.shape[0]
+    slabs = lax.axis_size("wide")
+    slab_here = lax.axis_index("wide")
+    slab_ids = jnp.arange(slabs, dtype=jnp.int32)
+    local = jnp.arange(rows_here, dtype=jnp.int32)
+    inverse = jnp.sum(jnp.where(slab_ids[:, None] == slab_table[None, :], local[None, :], 0), axis=1)
+    source = (2 * slab_here - slab_table) % slabs
+    x = relay(hidden, modulation, final_weight, noisy, sigma, inverse, source, slabs)
+    height = 2 * rows_here
+    g = conv1_weight.reshape(3, 3 * conv1_weight.shape[1], conv1_weight.shape[2])
+    tops = slab_here * height + 2 * CHUNK * jnp.arange(rows_here // CHUNK + 1, dtype=jnp.int32)
+    masks = jnp.stack([tops % WPIX != 0, (tops + 2 * CHUNK) % WPIX != 0]).astype(f32)
+    return tuple(decode(masks, x, conv_in_weight, conv_in_bias, g, conv1_bias, height))
+
+
+def edge_masks(first_row, count, height):
+    global_rows = first_row + jnp.arange(count, dtype=jnp.int32)
+    upper = (global_rows % height != 0).astype(f32)
+    lower = (global_rows % height != height - 1).astype(f32)
+    return (upper, jnp.ones_like(upper), lower)
+
+
+def split_padded(value, sides, width):
     for axis, dim in sides:
         count, length = (lax.axis_size(axis), value.shape[dim])
         up = [(i, (i + 1) % count) for i in range(count - 1)]
@@ -24,13 +374,6 @@
         after = lax.ppermute(first, axis, down)
         value = jnp.concatenate([before, value, after], axis=dim)
     return value
-
-
-def edge_masks(first_row, count, height):
-    global_rows = first_row + jnp.arange(count, dtype=jnp.int32)
-    upper = (global_rows % height != 0).astype(jnp.float32)
-    lower = (global_rows % height != height - 1).astype(jnp.float32)
-    return (upper, jnp.ones_like(upper), lower)
 
 
 def conv_input_rows(latent, weight, bias, first_row, count, channels):
@@ -65,7 +408,7 @@
     return total
 
 
-def shards(
+def split_shards(
     hidden,
     modulation,
     final_weight,
@@ -110,7 +453,7 @@
         .reshape(2 * rows_here, 4 * grid_side * channels // 2)
     )
     depth = 2
-    latent = padded_2(pixel_rows, (("wide", 0),), depth)
+    latent = split_padded(pixel_rows, (("wide", 0),), depth)
     slab_height = 2 * rows_here
     conv_rows = slab_height + 2 * (depth - 1)
     first_conv = slab_here * slab_height - (depth - 1)
@@ -132,8 +475,9 @@
 
 
 def solution(mesh):
+    whole_channels = mesh.shape["tensor"] == 1
     return jax.shard_map(
-        shards,
+        shards if whole_channels else split_shards,
         mesh=mesh,
         in_specs=(
             P("wide", "tensor"),

time: 171 us -> 72.1 us (0.42); the launches traced: 168 us -> 71.8 us
  matrix products: 108 us -> 0 us
  Pallas kernels: 0 us -> 60.9 us
  local copies, waits for them, and re-layouts: 27.7 us -> 7.57 us
  starting transfers between devices: 10.6 us -> 0 us
  waiting for transfers between devices: 10.5 us -> 0 us
  other arithmetic: 9.59 us -> 2.01 us
    dot_general x13 -> x0, matrix products: 108 us -> none  [the longest x9 87.9 us: conv_three(): jnp.einsum('rkw,ko->row', window, weights[3 * row_off + col_off], preferr...]
    pallas_call x0 -> x2, Pallas kernels: none -> 60.9 us  [the longest x1 38.4 us: decode(): pl.pallas_call(decode_kernel, grid=(steps + 1,), in_specs=[pl.BlockSpec(m...]
    unnamed x25 -> x9, local copies, waits for them, and re-layouts: 18.7 us -> 7.57 us
    all_to_all x1 -> x0, waiting for transfers between devices: 10.5 us -> none  [shards(): lax.all_to_all(sendbuf, 'wide', split_axis=0, concat_axis=0, tiled=True)]
    all_to_all x1 -> x0, starting transfers between devices: 7.3 us -> none  [shards(): lax.all_to_all(sendbuf, 'wide', split_axis=0, concat_axis=0, tiled=True)]
    reduce_sum x1, other arithmetic: 6.74 us -> 0.74 us  [shards(): jnp.sum(jnp.where(slab_ids[:, None] == slab_table[None, :], local[None, :...]
    slice x6 -> x0, local copies, waits for them, and re-layouts: 3.87 us -> none  [the longest x1 3.43 us: shards(): decoder_features = features[depth - 1:depth - 1 + slab_height]]
    ppermute x2 -> x0, starting transfers between devices: 3.28 us -> none  [the longest x1 1.81 us: padded_2(): before = lax.ppermute(last, axis, up)]
  transfers between devices with their start and end apart: 3 -> 0, of which waited for: 1 -> 0; matrix products, arithmetic and copies ran while one was open for 2% -> 0% of each run, Pallas kernels for 0% -> 0%
where the time goes in v2:
time: 72.1 us; the launch traced here: 71.8 us
  Pallas kernels  60.9 us (84%)
  local copies, waits for them, and re-layouts  7.57 us (10%)
  other arithmetic  2.01 us (3%)
  between operations  1.36 us (2%)
    pallas_call x1, Pallas kernels, decode(): pl.pallas_call(decode_kernel, grid=(steps + 1,), in_specs=[pl.BlockSpec(m...  38.4 us
    pallas_call x1, Pallas kernels, relay(): pl.pallas_call(functools.partial(relay_kernel, slabs, features), grid=(to...  22.4 us
    unnamed x9, local copies, waits for them, and re-layouts  7.57 us

profile of v2, /device:TPU:0, one launch (start us, length us, event | category | flops | bytes accessed | tf_op | source)
XLA Modules:
  0.0 71.8 jit_solution(13808021223398924234)
XLA Ops:
  1.3 0.7 and_select_fusion.src_ref
  2.0 0.7 %select_reduce_fusion.inv_ref = s32[32]{0:T(128)S(1)} fusion(s32[24]{0:T(128)} %param.16), kind=kLoop, calls=%fused_computation | loop fusion | flops 2272 | bytes 224 | tf_op jit(solution)/shard_map/reduce_sum | solution.py:349
  2.8 0.6 add_convert_fusion.mask_ref
  3.3 1.3 %copy.14.noisy_ref = f32[1536,64]{1,0:T(8,128)S(1)} copy(f32[1536,64]{0,1:T(8,128)} %param.14) | data formatting | bytes 786432 | tf_op args[3]
  4.6 0.0 copy-start
  4.6 3.7 %copy-done = bf16[1536,3072]{1,0:T(8,128)(2,1)S(1)} copy-done((bf16[1536,3072]{1,0:T(8,128)(2,1)S(1)}, bf16[1536,3072]{1,0:T(8,128)(2,1)}, u32[]{:S(2)}) %copy-start) | copy-done | bytes 9437208
  8.3 0.0 copy-start.2
  8.3 1.0 %copy-done.2 = bf16[3072,64]{0,1:T(8,128)(2,1)S(1)} copy-done((bf16[3072,64]{0,1:T(8,128)(2,1)S(1)}, bf16[3072,64]{0,1:T(8,128)(2,1)}, u32[]{:S(2)}) %copy-start.2) | copy-done | bytes 393240
  9.3 0.0 copy-start.3
  9.3 0.7 %copy-done.3 = f32[2,3072]{1,0:T(2,128)S(1)} copy-done((f32[2,3072]{1,0:T(2,128)S(1)}, f32[2,3072]{1,0:T(2,128)}, u32[]{:S(2)}) %copy-start.3) | copy-done | bytes 24600
  10.0 22.4 %relay.1.x_ref = bf16[1664,256]{1,0:T(8,128)(2,1)S(1)} custom-call(s32[32]{0:T(128)S(1)} %select_reduce_fusion.inv_ref, s32[24]{0:T(128)S(1)} %and_select_fusion.src_ref, f32[1,64]{1,0:T(1,128)S(1)} %broadcast_in_dim.26.sigma_ref, f32[2,3072]{1,0:T(2,128)S(1)} %copy-done.3, bf16[64,3072]{1,0:T(8,128)(2,1)S(1)} %bitcast.5, bf16[1536,3072]{1,0:T(8,128)(2,1)S(1)} %copy-done, ...), custom_call_target="tpu_custom_call" | custom-call | flops 2415919104 | bytes 9437184 | tf_op jit(solution)/shard_map/relay/pallas_call | solution.py:150
  32.5 0.0 copy-start.1
  32.5 0.9 %copy-done.1 = bf16[1664,256]{1,0:T(8,128)(2,1)} copy-done((bf16[1664,256]{1,0:T(8,128)(2,1)}, bf16[1664,256]{1,0:T(8,128)(2,1)S(1)}, u32[]{:S(2)}) %copy-start.1) | copy-done | bytes 851992
  33.4 38.4 %decode.1 = (bf16[48,512,128]{2,1,0:T(8,128)(2,1)}, bf16[48,512,128]{2,1,0:T(8,128)(2,1)}) custom-call(f32[2,7]{1,0:T(2,128)} %add_convert_fusion.mask_ref, bf16[1664,256]{1,0:T(8,128)(2,1)} %copy-done.1, bf16[1024,144]{1,0:T(8,128)(2,1)} %constant.61.clone.spread_ref, bf16[144,512]{1,0:T(8,128)(2,1)} %win_ref.1, f32[1,512]{1,0:T(1,128)} %bitcast.7, ...), custom_call_target="tpu_custom_call" | custom-call | flops 19327352832 | bytes 31457280 | tf_op jit(solution)/shard_map/decode/pallas_call | solution.py:309
  (2 shorter events, 0.0 us)
Async XLA Ops:
  4.6 3.7 %copy-start = (bf16[1536,3072]{1,0:T(8,128)(2,1)S(1)}, bf16[1536,3072]{1,0:T(8,128)(2,1)}, u32[]{:S(2)}) copy-start(bf16[1536,3072]{1,0:T(8,128)(2,1)} %hidden_ref.1) | copy-start | bytes 28311556
  8.3 1.0 %copy-start.2 = (bf16[3072,64]{0,1:T(8,128)(2,1)S(1)}, bf16[3072,64]{0,1:T(8,128)(2,1)}, u32[]{:S(2)}) copy-start(bf16[3072,64]{0,1:T(8,128)(2,1)} %param.13) | copy-start | bytes 1179652
  9.3 0.7 %copy-start.3 = (f32[2,3072]{1,0:T(2,128)S(1)}, f32[2,3072]{1,0:T(2,128)}, u32[]{:S(2)}) copy-start(f32[2,3072]{1,0:T(2,128)} %mod_ref.1) | copy-start | bytes 73732
  32.5 0.9 %copy-start.1 = (bf16[1664,256]{1,0:T(8,128)(2,1)}, bf16[1664,256]{1,0:T(8,128)(2,1)S(1)}, u32[]{:S(2)}) copy-start(bf16[1664,256]{1,0:T(8,128)(2,1)S(1)} %relay.1.x_ref) | copy-start | bytes 2555908

commit v3 on v2

--- a/solution.py
+++ b/solution.py
@@ -31,7 +31,7 @@
     return hi, mid, (rest - mid.astype(f32)).astype(bf16)
 
 
-def relay_kernel(slabs, features, inv_ref, src_ref, sigma_ref, mod_ref, wt_ref, hidden_ref, noisy_ref, x_ref, wcat, consts, rows, sendbuf, recv, ordered, halo, shifted, wide, send_sem, recv_sem, edge_send, edge_recv):
+def relay_kernel(slabs, features, inv_ref, table_ref, sigma_ref, mod_ref, wt_ref, hidden_ref, noisy_ref, g_ref, x_ref, mixed_ref, wcat, consts, rows, sendbuf, recv, ordered, halo, shifted, wide, send_sem, recv_sem, edge_send, edge_recv):
     step = pl.program_id(0)
     me = lax.axis_index("wide")
     values = wt_ref.shape[0]
@@ -64,7 +64,7 @@
     mean = acc[:, 3 * values : 3 * values + 1] / features
     rstd = 1.0 / jnp.sqrt(square / features - mean * mean + norm_eps)
     velocity = rstd * (hw - mean * consts[0:1, :]) + consts[1:2, :]
-    clean = noisy_ref[...] - sigma_ref[0:1, :] * velocity
+    clean = noisy_ref[...].T - sigma_ref[0:1, :] * velocity
     here = h.shape[0] // GRID
     for t in range(here):
         pair = [clean[t * GRID : t * GRID + HALF], clean[t * GRID + HALF : (t + 1) * GRID]]
@@ -89,10 +89,20 @@
             copy.start()
             copies.append(copy)
         recv[me] = sendbuf[me]
+
+        def mix(i, carry):
+            at = pl.ds(pl.multiple_of(i * 64, 64), 64)
+            outer = 0.5 * (g_ref[0, at, :].astype(f32) + g_ref[2, at, :].astype(f32))
+            inner = 0.5 * g_ref[1, at, :].astype(f32)
+            mixed_ref[0, at, :] = (outer + inner).astype(bf16)
+            mixed_ref[1, at, :] = (outer - inner).astype(bf16)
+            return carry
+
+        lax.fori_loop(0, g_ref.shape[1] // 64, mix, 0)
         for copy in copies:
             copy.wait_recv()
         for j in range(count):
-            ordered[j] = recv[src_ref[j]]
+            ordered[j] = recv[lax.rem(2 * me + slabs - table_ref[j], slabs)]
         edges = []
         for e, (row, peer) in enumerate(((count - 1, lax.rem(me + 1, slabs)), (0, lax.rem(me + slabs - 1, slabs)))):
             copy = pltpu.make_async_remote_copy(
@@ -140,10 +150,10 @@
             copy.wait_send()
 
 
-def relay(hidden, modulation, final_weight, noisy, sigma, inverse, source, slabs):
+def relay(hidden, modulation, final_weight, noisy, sigma, inverse, table, g, slabs):
     tokens, features = hidden.shape
     values = final_weight.shape[1]
-    count = source.shape[0]
+    count = table.shape[0]
     block = 256
     smem = pl.BlockSpec(memory_space=pltpu.SMEM)
     row = (HALF, 2 * values)
@@ -157,10 +167,17 @@
             pl.BlockSpec((2, features), lambda i: (0, 0)),
             pl.BlockSpec((values, features), lambda i: (0, 0)),
             pl.BlockSpec((block, features), lambda i: (i, 0)),
-            pl.BlockSpec((block, values), lambda i: (i, 0)),
-        ],
-        out_specs=pl.BlockSpec(((count + 2) * GRID, 4 * values), lambda i: (0, 0)),
-        out_shape=jax.ShapeDtypeStruct(((count + 2) * GRID, 4 * values), bf16),
+            pl.BlockSpec((values, block), lambda i: (0, i)),
+            pl.BlockSpec(g.shape, lambda i: (0, 0, 0), pipeline_mode=pl.Buffered(1)),
+        ],
+        out_specs=[
+            pl.BlockSpec(((count + 2) * GRID, 4 * values), lambda i: (0, 0)),
+            pl.BlockSpec((2,) + g.shape[1:], lambda i: (0, 0, 0)),
+        ],
+        out_shape=[
+            jax.ShapeDtypeStruct(((count + 2) * GRID, 4 * values), bf16),
+            jax.ShapeDtypeStruct((2,) + g.shape[1:], bf16),
+        ],
         scratch_shapes=[
             pltpu.VMEM((4 * values, features), bf16),
             pltpu.VMEM((8, values), f32),
@@ -176,10 +193,10 @@
             pltpu.SemaphoreType.DMA((2,)),
             pltpu.SemaphoreType.DMA((2,)),
         ],
-        compiler_params=pltpu.CompilerParams(vmem_limit_bytes=40 << 20, collective_id=0, has_side_effects=True),
+        compiler_params=pltpu.CompilerParams(vmem_limit_bytes=60 << 20, collective_id=0, has_side_effects=True),
         cost_estimate=pl.CostEstimate(flops=2 * tokens * features * 256, bytes_accessed=2 * tokens * features, transcendentals=0),
         name="relay",
-    )(inverse, source, jnp.broadcast_to(sigma, (1, values)), modulation, final_weight.T, hidden, noisy)
+    )(inverse, table, jnp.broadcast_to(sigma, (1, values)), modulation, final_weight.T, hidden, noisy.T, g)
 
 
 def spread_table():
@@ -196,7 +213,7 @@
     return table.reshape(-1, 9 * LC)
 
 
-def decode_kernel(mask_ref, x_ref, spread_ref, win_ref, bin_ref, g_ref, b1_ref, feat_ref, res_ref, wbig, mixed, nat, pad, act, tr_a, tr_b):
+def decode_kernel(x_ref, spread_ref, win_ref, bin_ref, g_ref, mixed, b1_ref, feat_ref, res_ref, wbig, nat, pad, act, tr_a, tr_b):
     step = pl.program_id(0)
     last = pl.num_programs(0) - 1
     chans = win_ref.shape[1]
@@ -211,18 +228,13 @@
             part = spread_ref[pixel * patch : (pixel + 1) * patch, :]
             wbig[pixel] = jnp.dot(part, win_ref[...], preferred_element_type=f32).astype(bf16)
 
-        def mix(i, carry):
-            at = pl.ds(pl.multiple_of(i * 64, 64), 64)
-            outer = 0.5 * (g_ref[0, at, :].astype(f32) + g_ref[2, at, :].astype(f32))
-            inner = 0.5 * g_ref[1, at, :].astype(f32)
-            mixed[0, at, :] = (outer + inner).astype(bf16)
-            mixed[1, at, :] = (outer - inner).astype(bf16)
-            return carry
-
-        lax.fori_loop(0, g_ref.shape[1] // 64, mix, 0)
-
     def prepare(tr):
         base = step * CHUNK * GRID
+        top = lax.axis_index("wide") * (last * pixel_rows) + step * pixel_rows
+        edge = {
+            0: jnp.where(lax.rem(top, WPIX) != 0, 1.0, 0.0).astype(f32),
+            pixel_rows + 1: jnp.where(lax.rem(top + pixel_rows, WPIX) != 0, 1.0, 0.0).astype(f32),
+        }
 
         def first(start, length, pixel):
             x = x_ref[pl.ds(pl.multiple_of(start, GRID), length), :]
@@ -233,28 +245,29 @@
             for c in range(chans // 128):
                 nat[row, c, pl.ds(b, GRID, stride=2), :] = f[:, c * 128 : (c + 1) * 128]
 
-        for b in range(2):
+        def ends(b):
             keep(first(base, GRID, 2 + b), 0, b)
             keep(first(base + (CHUNK + 1) * GRID, GRID, b), pixel_rows + 1, b)
-        for pixel in range(4):
+
+        def middle(pixel):
             f = first(base + GRID, CHUNK * GRID, pixel)
             for t in range(CHUNK):
                 keep(f[t * GRID : (t + 1) * GRID], 1 + 2 * t + pixel // 2, pixel % 2)
-        for r in range(pixel_rows + 2):
+
+        def activate(r):
             f = jnp.concatenate([nat[r, c] for c in range(chans // 128)], axis=1)
             if 1 <= r <= pixel_rows:
                 feat_ref[r - 1] = f.astype(bf16).T
             half = 0.5 * f
             a = half + half * jnp.tanh(half)
-            if r == 0:
-                a = a * mask_ref[0, step]
-            if r == pixel_rows + 1:
-                a = a * mask_ref[1, step]
+            if r in edge:
+                a = a * edge[r]
             pad[r, 8 : 8 + WPIX, :] = a
             act[r, :, chans : 2 * chans] = a.astype(bf16)
             act[r, :, 0:chans] = pad[r, 7 : 7 + WPIX, :].astype(bf16)
             act[r, :, 2 * chans :] = pad[r, 9 : 9 + WPIX, :].astype(bf16)
-        for p in range(CHUNK):
+
+        def combine(p):
             at = slice(p * WPIX, (p + 1) * WPIX)
             d = [act[2 * p + i] for i in range(4)]
             tr[0, at, :] = d[0] - d[2]
@@ -262,44 +275,68 @@
             tr[2, at, :] = d[2] - d[1]
             tr[3, at, :] = d[1] - d[3]
 
-    def residual(tr):
+        call = functools.partial
+        parts = [call(ends, b) for b in range(2)] + [call(middle, pixel) for pixel in range(4)]
+        for r in range(pixel_rows + 2):
+            parts.append(call(activate, r))
+            if r >= 3 and r % 2 == 1:
+                parts.append(call(combine, (r - 3) // 2))
+        return parts
+
+    def residual(tr, parts):
+        done = 0
+        total = 2 * (chans // tile) * (CHUNK * 2)
+        slot = 0
+
+        def between():
+            nonlocal done, slot
+            slot += 1
+            while done * total < slot * len(parts) and done < len(parts):
+                parts[done]()
+                done += 1
+
         for n in range(chans // tile):
             cols = slice(n * tile, (n + 1) * tile)
             bias = b1_ref[:, cols]
             factors = (g_ref[0, :, cols], mixed[0, :, cols], mixed[1, :, cols], g_ref[2, :, cols])
-            m = [jnp.dot(tr[k], factors[k], preferred_element_type=f32) for k in range(4)]
+            m = []
+            for k in range(4):
+                m.append(jnp.dot(tr[k], factors[k], preferred_element_type=f32))
+                between()
+                between()
             y0 = m[0] + (m[1] + m[2]) + bias
             y1 = (m[1] - m[2]) - m[3] + bias
             for p in range(CHUNK):
                 at = slice(p * WPIX, (p + 1) * WPIX)
                 res_ref[2 * p, cols, :] = y0[at].astype(bf16).T
+                between()
                 res_ref[2 * p + 1, cols, :] = y1[at].astype(bf16).T
+                between()
 
     @pl.when(step == 0)
     def _():
         setup()
-        prepare(tr_a)
+        for part in prepare(tr_a):
+            part()
 
     @pl.when((step > 0) & (step < last) & (lax.rem(step, 2) == 1))
     def _():
-        residual(tr_a)
-        prepare(tr_b)
+        residual(tr_a, prepare(tr_b))
 
     @pl.when((step > 0) & (step < last) & (lax.rem(step, 2) == 0))
     def _():
-        residual(tr_b)
-        prepare(tr_a)
+        residual(tr_b, prepare(tr_a))
 
     @pl.when((step == last) & (lax.rem(step, 2) == 1))
     def _():
-        residual(tr_a)
+        residual(tr_a, [])
 
     @pl.when((step == last) & (lax.rem(step, 2) == 0))
     def _():
-        residual(tr_b)
-
-
-def decode(masks, x, win, b_in, g, b1, height):
+        residual(tr_b, [])
+
+
+def decode(x, win, b_in, g, mixed, b1, height):
     chans = win.shape[1]
     rows = 2 * CHUNK
     steps = height // rows
@@ -310,12 +347,12 @@
         decode_kernel,
         grid=(steps + 1,),
         in_specs=[
-            pl.BlockSpec(memory_space=pltpu.SMEM),
             whole(*x.shape),
             whole(*spread.shape),
             whole(*win.shape),
             whole(1, chans),
             whole(*g.shape),
+            whole(*mixed.shape),
             whole(1, chans),
         ],
         out_specs=[
@@ -325,7 +362,6 @@
         out_shape=[shape, shape],
         scratch_shapes=[
             pltpu.VMEM((4, x.shape[1], chans), bf16),
-            pltpu.VMEM((2,) + g.shape[1:], bf16),
             pltpu.VMEM((rows + 2, chans // 128, WPIX, 128), f32),
             pltpu.VMEM((rows + 2, WPIX + 16, chans), f32),
             pltpu.VMEM((rows + 2, WPIX, 3 * chans), bf16),
@@ -335,7 +371,7 @@
         compiler_params=pltpu.CompilerParams(vmem_limit_bytes=60 << 20),
         cost_estimate=pl.CostEstimate(flops=height * WPIX * 12 * 512 * 512, bytes_accessed=30 << 20, transcendentals=0),
         name="decode",
-    )(masks, x, spread, win, b_in[None], g, b1[None])
+    )(x, spread, win, b_in[None], g, mixed, b1[None])
 
 
 def shards(hidden, modulation, final_weight, noisy, step_index, slab_table, conv_in_weight, conv_in_bias, conv1_weight, conv1_bias):
@@ -343,17 +379,13 @@
     sigma = shift_value * frac / (1.0 + (shift_value - 1.0) * frac)
     rows_here = slab_table.shape[0]
     slabs = lax.axis_size("wide")
-    slab_here = lax.axis_index("wide")
     slab_ids = jnp.arange(slabs, dtype=jnp.int32)
     local = jnp.arange(rows_here, dtype=jnp.int32)
     inverse = jnp.sum(jnp.where(slab_ids[:, None] == slab_table[None, :], local[None, :], 0), axis=1)
-    source = (2 * slab_here - slab_table) % slabs
-    x = relay(hidden, modulation, final_weight, noisy, sigma, inverse, source, slabs)
+    g = conv1_weight.reshape(3, 3 * conv1_weight.shape[1], conv1_weight.shape[2])
+    x, mixed = relay(hidden, modulation, final_weight, noisy, sigma, inverse, slab_table, g, slabs)
     height = 2 * rows_here
-    g = conv1_weight.reshape(3, 3 * conv1_weight.shape[1], conv1_weight.shape[2])
-    tops = slab_here * height + 2 * CHUNK * jnp.arange(rows_here // CHUNK + 1, dtype=jnp.int32)
-    masks = jnp.stack([tops % WPIX != 0, (tops + 2 * CHUNK) % WPIX != 0]).astype(f32)
-    return tuple(decode(masks, x, conv_in_weight, conv_in_bias, g, conv1_bias, height))
+    return tuple(decode(x, conv_in_weight, conv_in_bias, g, mixed, conv1_bias, height))
 
 
 def edge_masks(first_row, count, height):

time: 72.1 us -> 69 us (0.957)
  local copies, waits for them, and re-layouts: 7.57 us -> 0.51 us
  Pallas kernels: 60.9 us -> 65.7 us
  other arithmetic: 2.01 us -> 1.25 us
    unnamed x9 -> x0, local copies, waits for them, and re-layouts: 7.57 us -> none
    pallas_call x1, Pallas kernels: 22.4 us -> 28.2 us  [relay(): pl.pallas_call(functools.partial(relay_kernel, slabs, features), grid=(to...]
    pallas_call x1, Pallas kernels: 38.4 us -> 37.5 us  [decode(): pl.pallas_call(decode_kernel, grid=(steps + 1,), in_specs=[whole(*x.shape...]
where the time goes in v3:
time: 69 us; the launch traced here: 68.8 us
  Pallas kernels  65.7 us (95%)
  between operations  1.33 us (2%)
  other arithmetic  1.25 us (2%)
    pallas_call x1, Pallas kernels, decode(): pl.pallas_call(decode_kernel, grid=(steps + 1,), in_specs=[whole(*x.shape...  37.5 us
    pallas_call x1, Pallas kernels, relay(): pl.pallas_call(functools.partial(relay_kernel, slabs, features), grid=(to...  28.2 us

profile of v3, /device:TPU:0, one launch (start us, length us, event | category | flops | bytes accessed | tf_op | source)
XLA Modules:
  0.0 68.8 jit_solution(4271771631733533855)
XLA Ops:
  1.3 0.5 broadcast_in_dim.26.sigma_ref
  1.8 1.3 %select_reduce_fusion.inv_ref = s32[32]{0:T(128)} fusion(s32[24]{0:T(128)} %table_ref.1), kind=kLoop, calls=%fused_computation | loop fusion | flops 2272 | bytes 224 | tf_op jit(solution)/shard_map/reduce_sum | solution.py:384
  3.1 28.2 %relay.1 = (bf16[1664,256]{1,0:T(8,128)(2,1)}, bf16[2,1536,512]{2,1,0:T(8,128)(2,1)}) custom-call(s32[32]{0:T(128)} %select_reduce_fusion.inv_ref, s32[24]{0:T(128)} %table_ref.1, f32[1,64]{1,0:T(1,128)} %broadcast_in_dim.26.sigma_ref, f32[2,3072]{1,0:T(2,128)} %mod_ref.1, bf16[64,3072]{1,0:T(8,128)(2,1)} %bitcast.8, bf16[1536,3072]{1,0:T(8,128)(2,1)} %hidden_ref.1, ...), custom_call_target="tpu_custom_call" | custom-call | flops 2415919104 | bytes 9437184 | tf_op jit(solution)/shard_map/relay/pallas_call | solution.py:160
  31.3 37.5 %decode.1 = (bf16[48,512,128]{2,1,0:T(8,128)(2,1)}, bf16[48,512,128]{2,1,0:T(8,128)(2,1)}) custom-call(bf16[1664,256]{1,0:T(8,128)(2,1)} %get-tuple-element.4.x_ref, bf16[1024,144]{1,0:T(8,128)(2,1)} %constant.17.clone.spread_ref, bf16[144,512]{1,0:T(8,128)(2,1)} %win_ref.1, f32[1,512]{1,0:T(1,128)} %bitcast.10, bf16[3,1536,512]{2,1,0:T(8,128)(2,1)} %bitcast.7, ...), custom_call_target="tpu_custom_call" | custom-call | flops 19327352832 | bytes 31457280 | tf_op jit(solution)/shard_map/decode/pallas_call | solution.py:346
